TPU v7x, 32 devices: a whole 2x2x4 slice. The times are simulated.
32 devices in a mesh: dp: 4 (over y, x), blk: 8 (over z, core).
Axes of the slice: x: 2, y: 2, z: 4, core: 2. Of those that a mesh axis runs over, the one named last changes fastest.
Arguments:
- tokens: bfloat16 [8, 512, 1024], P('dp', 'blk'), may hold values from -6 to 6
- doc_ids: int32 [8, 512], P('dp', 'blk'), may hold values from 0 to 7, as said below
- w_query: float32 [1024, 1024], P(('dp', 'blk')), may hold values from -0.1875 to 0.1875
- w_key: float32 [1024, 1024], P(('dp', 'blk')), may hold values from -0.1875 to 0.1875
- w_value: float32 [1024, 1024], P(('dp', 'blk')), may hold values from -0.1875 to 0.1875
- w_out: float32 [1024, 1024], P(('dp', 'blk')), may hold values from -0.1875 to 0.1875
- w_up: float32 [1024, 4096], P(('dp', 'blk')), may hold values from -0.1875 to 0.1875
- w_gate: float32 [1024, 4096], P(('dp', 'blk')), may hold values from -0.1875 to 0.1875
- w_down: float32 [4096, 1024], P(('dp', 'blk')), may hold values from -0.09375 to 0.09375
- s_qk: float32 [1024], replicated, may hold values from 1 to 2
- alpha_attn: float32 [1024], replicated, may hold values from 0.2 to 0.8
- s_up: float32 [4096], replicated, may hold values from 0.5 to 2
- s_gate: float32 [4096], replicated, may hold values from 0.5 to 2
- alpha_mlp: float32 [1024], replicated, may hold values from 0.2 to 0.8
- cotangent: bfloat16 [8, 512, 1024], P('dp', 'blk'), may hold values from -6 to 6
Outputs:
- hidden_out: bfloat16 [8, 512, 1024], P('dp', 'blk')
- tokens_grad: float32 [8, 512, 1024], P('dp', 'blk')
- g_query: float32 [1024, 1024], P(('dp', 'blk'))
- g_key: float32 [1024, 1024], P(('dp', 'blk'))
- g_value: float32 [1024, 1024], P(('dp', 'blk'))
- g_out: float32 [1024, 1024], P(('dp', 'blk'))
- g_up: float32 [1024, 4096], P(('dp', 'blk'))
- g_gate: float32 [1024, 4096], P(('dp', 'blk'))
- g_down: float32 [4096, 1024], P(('dp', 'blk'))
- g_sqk: float32 [1024], P(('dp', 'blk'))
- g_alpha_attn: float32 [1024], P(('dp', 'blk'))
- g_s_up: float32 [4096], P(('dp', 'blk'))
- g_s_gate: float32 [4096], P(('dp', 'blk'))
- g_alpha_mlp: float32 [1024], P(('dp', 'blk'))
Inputs may be any that keep to these rules, and one draw needn't show every extreme that they name: `doc_ids`: along each row the ids never fall, and every id from 0 to 7 occurs in every row.
All inputs are finite; a program needn't handle non-finite values.
Results may differ from a plain program's by a relative error of at most 0.03.
Values may be sent and summed in bfloat16 or wider, within the bound.
No kernel may reach another device: no remote copies, remote signals or barrier semaphores. Data moves between devices by JAX's collectives and lax.ppermute only.
A program may use at most 320 MiB of HBM per device.

v0:
```python
import math

import jax
import jax.numpy as jnp
from jax import lax
from jax.sharding import PartitionSpec as P

HEADS = 16
HEAD_DIM = 64
NDOC = 8


epsilon = 1e-06
negative = -1e30


def prefix(part, axis, combine, identity):
    place = lax.axis_index(axis)
    gathered = lax.all_gather(part, axis)
    state = jnp.zeros_like(part) + jnp.asarray(identity, part.dtype)

    def one(lap, state):
        return combine(state, lax.dynamic_index_in_dim(gathered, lap, 0, False))

    return lax.fori_loop(0, place, one, state)


def rotate(tensor, cosines, sines):
    half_dim = tensor.shape[-1] // 2
    front = tensor[..., :half_dim]
    behind = tensor[..., half_dim:]
    return jnp.concatenate(
        [front * cosines - behind * sines, behind * cosines + front * sines], axis=-1
    )


def sphere(tensor):
    return tensor * lax.rsqrt(jnp.mean(tensor * tensor, axis=-1, keepdims=True) + epsilon)


def head_unit(tensor, gains):
    return gains * tensor * lax.rsqrt(jnp.sum(tensor * tensor, axis=-1, keepdims=True) + epsilon)


def rope_tables(positions):
    frequency = 10000.0 ** (-jnp.arange(HEAD_DIM // 2, dtype=jnp.float32) / (HEAD_DIM // 2))
    angles = positions.astype(jnp.float32)[..., None] * frequency
    return (jnp.cos(angles)[..., None, :], jnp.sin(angles)[..., None, :])


def combine_counts(earlier, later):
    return earlier + later


def residual_step(branch, residual_in, alpha):
    return sphere(residual_in + alpha * (sphere(branch) - residual_in))


def gating(up_proj, gate_proj, scale_up, scale_gate):
    return scale_up * up_proj * jax.nn.silu(scale_gate * gate_proj)


def allowed_mask(query_index, query_start, key_index):
    below = key_index[None, None, :] <= query_index[None, :, None]
    inside = key_index[None, None, :] >= query_start[:, :, None]
    return (below & inside)[:, None]


def split_heads(tensor):
    return tensor.reshape(tensor.shape[:-1] + (HEADS, HEAD_DIM))


def merge_heads(tensor):
    return tensor.reshape(tensor.shape[:-2] + (HEADS * HEAD_DIM,))


def outer_rows(left, right):
    return jnp.einsum("tr,tc->rc", left, right, preferred_element_type=jnp.float32)


def body(
    tokens,
    doc_ids,
    w_query,
    w_key,
    w_value,
    w_out,
    w_up,
    w_gate,
    w_down,
    s_qk,
    alpha_attn,
    s_up,
    s_gate,
    alpha_mlp,
    cotangent,
):
    num_seqs, seg_len, model_width = tokens.shape
    score_scale = math.sqrt(HEAD_DIM)
    onehot_docs = (doc_ids[..., None] == jnp.arange(NDOC, dtype=jnp.int32)).astype(jnp.int32)
    doc_counts = jnp.sum(onehot_docs, axis=1)
    earlier_counts = prefix(doc_counts, "blk", combine_counts, jnp.zeros_like(doc_counts))
    local_first = jnp.cumsum(doc_counts, axis=1) - doc_counts
    local_index = jnp.arange(seg_len, dtype=jnp.int32)
    positions = local_index[None, :] - jnp.sum(
        onehot_docs * (local_first - earlier_counts)[:, None, :], axis=2
    )
    global_index = lax.axis_index("blk") * seg_len + local_index
    doc_start = global_index[None, :] - positions
    cosines, sines = rope_tables(positions)
    full_query, full_key, full_value, full_out, full_up, full_gate, full_down = (
        lax.all_gather(w_query.astype(jnp.bfloat16), ("dp", "blk"), axis=0, tiled=True),
        lax.all_gather(w_key.astype(jnp.bfloat16), ("dp", "blk"), axis=0, tiled=True),
        lax.all_gather(w_value.astype(jnp.bfloat16), ("dp", "blk"), axis=0, tiled=True),
        lax.all_gather(w_out.astype(jnp.bfloat16), ("dp", "blk"), axis=0, tiled=True),
        lax.all_gather(w_up.astype(jnp.bfloat16), ("dp", "blk"), axis=0, tiled=True),
        lax.all_gather(w_gate.astype(jnp.bfloat16), ("dp", "blk"), axis=0, tiled=True),
        lax.all_gather(w_down.astype(jnp.bfloat16), ("dp", "blk"), axis=0, tiled=True),
    )
    flat_tokens = tokens.reshape(num_seqs * seg_len, model_width)
    token_rows = flat_tokens.astype(jnp.float32)
    q_pre = jnp.dot(flat_tokens, full_query, preferred_element_type=jnp.float32).reshape(
        tokens.shape
    )
    k_pre = jnp.dot(flat_tokens, full_key, preferred_element_type=jnp.float32).reshape(tokens.shape)
    v_pre = jnp.dot(flat_tokens, full_value, preferred_element_type=jnp.float32).reshape(
        tokens.shape
    )

    def unit_pair(query_pre, key_pre, gains):
        head_gains = gains.reshape(HEADS, HEAD_DIM)
        query_heads = head_unit(rotate(split_heads(query_pre), cosines, sines), head_gains)
        key_heads = head_unit(rotate(split_heads(key_pre), cosines, sines), head_gains)
        return (merge_heads(query_heads), merge_heads(key_heads))

    (q_unit, k_unit), unit_pull = jax.vjp(unit_pair, q_pre, k_pre, s_qk)
    q_low = q_unit.astype(jnp.bfloat16)
    k_low = k_unit.astype(jnp.bfloat16)
    v_low = v_pre.astype(jnp.bfloat16)
    q_heads_low = split_heads(q_low)
    k_heads_local = split_heads(k_low)
    v_heads_local = split_heads(v_low)
    stat_shape = (num_seqs, HEADS, seg_len)
    zero_rows = jnp.zeros(tokens.shape, jnp.float32)
    row_peak = jnp.full(stat_shape, negative, jnp.float32)
    accum = zero_rows
    key_rows = lax.all_gather(k_low, "blk", axis=1, tiled=True)
    value_rows = lax.all_gather(v_low, "blk", axis=1, tiled=True)
    key_count = key_rows.shape[1]
    key_index = jnp.arange(key_count, dtype=jnp.int32)
    scores = (
        jnp.einsum(
            "bqhd,bkhd->bhqk",
            q_heads_low,
            split_heads(key_rows),
            preferred_element_type=jnp.float32,
        )
        * score_scale
    )
    allowed = allowed_mask(global_index, doc_start, key_index)
    scores = jnp.where(allowed, scores, negative)
    new_peak = jnp.maximum(row_peak, jnp.max(scores, axis=-1))
    factor = jnp.exp(row_peak - new_peak)
    weights_now = jnp.where(allowed, jnp.exp(scores - new_peak[..., None]), 0.0)
    denominator = jnp.sum(weights_now, axis=-1)
    update = jnp.einsum(
        "bhqk,bkhd->bqhd",
        weights_now.astype(jnp.bfloat16),
        split_heads(value_rows),
        preferred_element_type=jnp.float32,
    )
    accum = split_heads(accum) * jnp.swapaxes(factor, 1, 2)[..., None] + update
    row_peak, denominator, accum = (new_peak, denominator, merge_heads(accum))
    log_total = row_peak + jnp.log(denominator)
    attended = merge_heads(split_heads(accum) / jnp.swapaxes(denominator, 1, 2)[..., None])
    attended_low = attended.astype(jnp.bfloat16)
    flat_attended = attended_low.reshape(-1, model_width)
    h_attn = jnp.dot(flat_attended, full_out, preferred_element_type=jnp.float32)
    h_one, attn_pull = jax.vjp(residual_step, h_attn, token_rows, alpha_attn)
    h_low = h_one.astype(jnp.bfloat16)
    up_proj = jnp.dot(h_low, full_up, preferred_element_type=jnp.float32)
    gate_proj = jnp.dot(h_low, full_gate, preferred_element_type=jnp.float32)
    mixed, gate_pull = jax.vjp(gating, up_proj, gate_proj, s_up, s_gate)
    mixed_low = mixed.astype(jnp.bfloat16)
    h_mlp = jnp.dot(mixed_low, full_down, preferred_element_type=jnp.float32)
    result, out_pull = jax.vjp(residual_step, h_mlp, h_one, alpha_mlp)
    hidden_out = result.astype(jnp.bfloat16).reshape(tokens.shape)
    back_query, back_key, back_value, back_out, back_up, back_gate, back_down = (
        lax.all_gather(w_query.astype(jnp.bfloat16), ("dp", "blk"), axis=0, tiled=True),
        lax.all_gather(w_key.astype(jnp.bfloat16), ("dp", "blk"), axis=0, tiled=True),
        lax.all_gather(w_value.astype(jnp.bfloat16), ("dp", "blk"), axis=0, tiled=True),
        lax.all_gather(w_out.astype(jnp.bfloat16), ("dp", "blk"), axis=0, tiled=True),
        lax.all_gather(w_up.astype(jnp.bfloat16), ("dp", "blk"), axis=0, tiled=True),
        lax.all_gather(w_gate.astype(jnp.bfloat16), ("dp", "blk"), axis=0, tiled=True),
        lax.all_gather(w_down.astype(jnp.bfloat16), ("dp", "blk"), axis=0, tiled=True),
    )
    d_result = cotangent.reshape(-1, model_width).astype(jnp.float32)
    d_hmlp, d_hone, g_alpha_mlp = out_pull(d_result)
    dm_low = d_hmlp.astype(jnp.bfloat16)
    sum_down = lax.psum_scatter(
        outer_rows(mixed_low, dm_low), ("dp", "blk"), scatter_dimension=0, tiled=True
    )
    d_mixed = jnp.einsum("td,fd->tf", dm_low, back_down, preferred_element_type=jnp.float32)
    d_up, d_gate, g_s_up, g_s_gate = gate_pull(d_mixed)
    du_low = d_up.astype(jnp.bfloat16)
    dg_low = d_gate.astype(jnp.bfloat16)
    d_hone = (
        d_hone
        + jnp.einsum("tf,df->td", du_low, back_up, preferred_element_type=jnp.float32)
        + jnp.einsum("tf,df->td", dg_low, back_gate, preferred_element_type=jnp.float32)
    )
    d_hattn, d_tokens, g_alpha_attn = attn_pull(d_hone)
    dh_low = d_hattn.astype(jnp.bfloat16)
    d_attended = (
        jnp.einsum("tj,ij->ti", dh_low, back_out, preferred_element_type=jnp.float32)
        .astype(jnp.bfloat16)
        .reshape(tokens.shape)
    )
    d_attn_heads = split_heads(d_attended)
    delta = jnp.swapaxes(
        jnp.sum(d_attn_heads.astype(jnp.float32) * split_heads(attended), axis=-1), 1, 2
    )
    log_all, delta_all, start_all = (
        lax.all_gather(log_total, "blk", axis=2, tiled=True),
        lax.all_gather(delta, "blk", axis=2, tiled=True),
        lax.all_gather(doc_start.astype(jnp.float32), "blk", axis=1, tiled=True),
    )
    key_rows = lax.all_gather(k_low, "blk", axis=1, tiled=True)
    value_rows = lax.all_gather(v_low, "blk", axis=1, tiled=True)
    key_count = key_rows.shape[1]
    key_index = jnp.arange(key_count, dtype=jnp.int32)
    key_heads = split_heads(key_rows)
    scores = (
        jnp.einsum("bqhd,bkhd->bhqk", q_heads_low, key_heads, preferred_element_type=jnp.float32)
        * score_scale
    )
    allowed = allowed_mask(global_index, doc_start, key_index)
    probs_now = jnp.where(
        allowed, jnp.exp(jnp.where(allowed, scores, negative) - log_total[..., None]), 0.0
    )
    d_probs = jnp.einsum(
        "bqhd,bkhd->bhqk", d_attn_heads, split_heads(value_rows), preferred_element_type=jnp.float32
    )
    d_scores = (probs_now * (d_probs - delta[..., None])).astype(jnp.bfloat16)
    update = jnp.einsum("bhqk,bkhd->bqhd", d_scores, key_heads, preferred_element_type=jnp.float32)
    d_query = score_scale * merge_heads(update)
    query_rows = lax.all_gather(q_low, "blk", axis=1, tiled=True)
    grad_rows = lax.all_gather(d_attended, "blk", axis=1, tiled=True)
    query_count = query_rows.shape[1]
    query_index = jnp.arange(query_count, dtype=jnp.int32)
    query_start = start_all.astype(jnp.int32)
    query_heads = split_heads(query_rows)
    grad_heads = split_heads(grad_rows)
    scores = (
        jnp.einsum(
            "bqhd,bkhd->bhqk", query_heads, k_heads_local, preferred_element_type=jnp.float32
        )
        * score_scale
    )
    allowed = allowed_mask(query_index, query_start, global_index)
    probs_now = jnp.where(
        allowed, jnp.exp(jnp.where(allowed, scores, negative) - log_all[..., None]), 0.0
    )
    value_update = jnp.einsum(
        "bhqk,bqhd->bkhd",
        probs_now.astype(jnp.bfloat16),
        grad_heads,
        preferred_element_type=jnp.float32,
    )
    d_probs = jnp.einsum(
        "bqhd,bkhd->bhqk", grad_heads, v_heads_local, preferred_element_type=jnp.float32
    )
    d_scores = (probs_now * (d_probs - delta_all[..., None])).astype(jnp.bfloat16)
    key_update = jnp.einsum(
        "bhqk,bqhd->bkhd", d_scores, query_heads, preferred_element_type=jnp.float32
    )
    d_keys = score_scale * merge_heads(key_update)
    d_values = merge_heads(value_update)
    d_qpre, d_kpre, g_sqk = unit_pull((d_query, d_keys))
    dq_low = d_qpre.astype(jnp.bfloat16).reshape(-1, model_width)
    dk_low = d_kpre.astype(jnp.bfloat16).reshape(-1, model_width)
    dv_low = d_values.astype(jnp.bfloat16).reshape(-1, model_width)
    d_tokens = d_tokens + jnp.einsum(
        "te,de->td", dq_low, back_query, preferred_element_type=jnp.float32
    )
    d_tokens = d_tokens + jnp.einsum(
        "te,de->td", dk_low, back_key, preferred_element_type=jnp.float32
    )
    d_tokens = d_tokens + jnp.einsum(
        "te,de->td", dv_low, back_value, preferred_element_type=jnp.float32
    )
    tokens_grad = d_tokens.reshape(tokens.shape)
    all_sums = lax.psum_scatter(
        jnp.concatenate(
            [
                jnp.concatenate(
                    [
                        outer_rows(flat_tokens, dq_low),
                        outer_rows(flat_tokens, dk_low),
                        outer_rows(flat_tokens, dv_low),
                        outer_rows(flat_attended, dh_low),
                    ],
                    axis=1,
                ),
                jnp.concatenate([outer_rows(h_low, du_low), outer_rows(h_low, dg_low)], axis=1),
            ],
            axis=1,
        ),
        ("dp", "blk"),
        scatter_dimension=0,
        tiled=True,
    )
    attn_sums = all_sums[:, : 4 * model_width]
    mlp_sums = all_sums[:, 4 * model_width :]
    sum_query = attn_sums[:, :model_width]
    sum_key = attn_sums[:, model_width : 2 * model_width]
    sum_value = attn_sums[:, 2 * model_width : 3 * model_width]
    sum_out = attn_sums[:, 3 * model_width :]
    hidden_units = full_up.shape[1]
    sum_up = mlp_sums[:, :hidden_units]
    sum_gate = mlp_sums[:, hidden_units:]
    sum_sqk, sum_alpha_attn, sum_s_up, sum_s_gate, sum_alpha_mlp = (
        lax.psum_scatter(g_sqk, ("dp", "blk"), scatter_dimension=0, tiled=True),
        lax.psum_scatter(g_alpha_attn, ("dp", "blk"), scatter_dimension=0, tiled=True),
        lax.psum_scatter(g_s_up, ("dp", "blk"), scatter_dimension=0, tiled=True),
        lax.psum_scatter(g_s_gate, ("dp", "blk"), scatter_dimension=0, tiled=True),
        lax.psum_scatter(g_alpha_mlp, ("dp", "blk"), scatter_dimension=0, tiled=True),
    )
    return (
        hidden_out,
        tokens_grad,
        sum_query,
        sum_key,
        sum_value,
        sum_out,
        sum_up,
        sum_gate,
        sum_down,
        sum_sqk,
        sum_alpha_attn,
        sum_s_up,
        sum_s_gate,
        sum_alpha_mlp,
    )


def solution(mesh):
    placed = (
        P("dp", "blk", None),
        P("dp", "blk"),
        P(("dp", "blk"), None),
        P(("dp", "blk"), None),
        P(("dp", "blk"), None),
        P(("dp", "blk"), None),
        P(("dp", "blk"), None),
        P(("dp", "blk"), None),
        P(("dp", "blk"), None),
        P(),
        P(),
        P(),
        P(),
        P(),
        P("dp", "blk", None),
    )
    return jax.shard_map(
        body,
        mesh=mesh,
        in_specs=placed,
        out_specs=(
            P("dp", "blk", None),
            P("dp", "blk", None),
            P(("dp", "blk"), None),
            P(("dp", "blk"), None),
            P(("dp", "blk"), None),
            P(("dp", "blk"), None),
            P(("dp", "blk"), None),
            P(("dp", "blk"), None),
            P(("dp", "blk"), None),
            P(("dp", "blk")),
            P(("dp", "blk")),
            P(("dp", "blk")),
            P(("dp", "blk")),
            P(("dp", "blk")),
        ),
        check_vma=False,
    )
```

profile of v0, /device:TPU:0, one launch (start us, length us, event | category | flops | bytes accessed | tf_op | source)
XLA Modules:
  0.0 1349.7 jit_solution(5671615110069255248)
XLA Ops:
  13.1 13.4 all-gather.1
  28.1 42.7 %all-gather.15.cloned.1.call-done = bf16[1024,1024]{1,0:T(8,128)(2,1)} async-done(((bf16[32,1024]{1,0:T(8,128)(2,1)}), bf16[1024,1024]{1,0:T(8,128)(2,1)}) %all-gather.15.cloned.1.call-update) | async-done | bytes 2097168 | tf_op jit(solution)/shard_map/all_gather | solution.py:112
  73.7 56.0 %all-gather.17.cloned.1.call-done = bf16[1024,1024]{1,0:T(8,128)(2,1)} async-done(((bf16[32,1024]{1,0:T(8,128)(2,1)}), bf16[1024,1024]{1,0:T(8,128)(2,1)}) %all-gather.17.cloned.1.call-update) | async-done | bytes 2097168 | tf_op jit(solution)/shard_map/all_gather | solution.py:113
  153.0 35.6 %all-gather.21.cloned.1.call-done = bf16[1024,1024]{1,0:T(8,128)(2,1)} async-done(((bf16[32,1024]{1,0:T(8,128)(2,1)}), bf16[1024,1024]{1,0:T(8,128)(2,1)}) %all-gather.21.cloned.1.call-update) | async-done | bytes 2097168 | tf_op jit(solution)/shard_map/all_gather | solution.py:114
  199.5 19.1 %all-gather.19.cloned.1.call-done = bf16[2,512,1024]{2,0,1:T(2,128)(2,1)} async-done(((bf16[2,64,1024]{2,0,1:T(2,128)(2,1)}), bf16[2,512,1024]{2,0,1:T(2,128)(2,1)}) %all-gather.19.cloned.1.call-update) | async-done | bytes 2097168 | tf_op jit(solution)/shard_map/all_gather | solution.py:147
  218.7 6.1 copy.162
  231.6 17.7 %all-gather.23.cloned.1.call-done = bf16[2,512,1024]{2,1,0:T(8,128)(2,1)} async-done(((bf16[2,64,1024]{2,1,0:T(8,128)(2,1)}), bf16[2,512,1024]{2,1,0:T(8,128)(2,1)}) %all-gather.23.cloned.1.call-update) | async-done | bytes 2097168 | tf_op jit(solution)/shard_map/all_gather | solution.py:148
  253.2 5.3 fusion.76
  259.3 49.4 %all-gather.25.cloned.1.call-done = bf16[1024,1024]{1,0:T(8,128)(2,1)} async-done(((bf16[32,1024]{1,0:T(8,128)(2,1)}), bf16[1024,1024]{1,0:T(8,128)(2,1)}) %all-gather.25.cloned.1.call-update) | async-done | bytes 2097168 | tf_op jit(solution)/shard_map/all_gather | solution.py:115
  313.2 75.2 %all-gather.29.cloned.1.call-done = bf16[1024,4096]{1,0:T(8,128)(2,1)} async-done(((bf16[32,4096]{1,0:T(8,128)(2,1)}), bf16[1024,4096]{1,0:T(8,128)(2,1)}) %all-gather.29.cloned.1.call-update) | async-done | bytes 8388624 | tf_op jit(solution)/shard_map/all_gather | solution.py:117
  388.4 6.1 fusion.79
  394.5 73.5 %all-gather.27.cloned.1.call-done = bf16[1024,4096]{1,0:T(8,128)(2,1)} async-done(((bf16[32,4096]{1,0:T(8,128)(2,1)}), bf16[1024,4096]{1,0:T(8,128)(2,1)}) %all-gather.27.cloned.1.call-update) | async-done | bytes 8388624 | tf_op jit(solution)/shard_map/all_gather | solution.py:116
  468.0 7.5 multiply_convert_fusion.4
  475.5 71.5 %all-gather.31.cloned.1.call-done = bf16[4096,1024]{1,0:T(8,128)(2,1)} async-done(((bf16[128,1024]{1,0:T(8,128)(2,1)}), bf16[4096,1024]{1,0:T(8,128)(2,1)}) %all-gather.31.cloned.1.call-update) | async-done | bytes 8388624 | tf_op jit(solution)/shard_map/all_gather | solution.py:118
  547.1 5.2 multiply_reduce_fusion.15
  554.7 8.0 multiply_reduce_fusion
  562.7 6.8 convolution_add_fusion.4
  576.1 10.5 all-gather.2
  591.8 17.1 %all_gather.70 = f32[2,16,512]{1,0,2:T(2,128)S(1)} all-gather(f32[2,16,64]{1,0,2:T(2,128)S(1)} %copy.175), channel_id=1, replica_groups=mesh['dp'=4,'blk'=8] {'blk'}, dimensions={2}, use_global_device_ids=true | all-gather | bytes 73728 | tf_op jit(solution)/shard_map/all_gather | solution.py:224
  609.7 6.1 copy.172
  624.8 16.0 %all_gather.72 = f32[2,16,512]{1,0,2:T(2,128)} all-gather(f32[2,16,64]{1,0,2:T(2,128)S(1)} %copy.179), channel_id=1, replica_groups=mesh['dp'=4,'blk'=8] {'blk'}, dimensions={2}, use_global_device_ids=true | all-gather | bytes 73728 | tf_op jit(solution)/shard_map/all_gather | solution.py:225
  642.0 6.8 convolution_bitcast_fusion.4
  658.0 7.9 multiply_reduce_fusion.3
  671.3 5.3 copy.186
  684.3 5.4 copy.187
  692.4 5.6 copy.188
  708.2 8.2 convolution_dynamic-update-slice_fusion.1
  716.4 8.3 convolution_dynamic-update-slice_fusion
  726.0 11.2 fusion.80
  746.2 38.5 %all-reduce.9 = (f32[1024]{0:T(1024)S(1)}, f32[1024]{0:T(1024)S(1)}, f32[4096]{0:T(1024)S(1)}, f32[4096]{0:T(1024)S(1)}, f32[1024]{0:T(1024)S(1)}) all-reduce(f32[1024]{0:T(1024)S(1)} %add_any.93, f32[1024]{0:T(1024)S(1)} %copy-done.42, f32[4096]{0:T(1024)S(1)} %copy-done.44, ...), channel_id=5, replica_groups=mesh['dp'=4,'blk'=8] {'dp','blk'}, use_global_device_ids=true, to_apply=%region_24.25.clone | all-reduce | flops 11264 | bytes 90112
  792.1 362.1 %reduce-scatter.3.cloned.1.call-done = f32[32,12288]{1,0:T(8,128)} async-done(((f32[1024,12288]{1,0:T(8,128)}), f32[32,12288]{1,0:T(8,128)}) %reduce-scatter.3.cloned.1.call-update) | async-done | bytes 1572880 | tf_op jit(solution)/shard_map/reduce_scatter | solution.py:293
  1158.3 184.4 %reduce-scatter.5.cloned.1.call-done = f32[128,1024]{1,0:T(8,128)} async-done(((f32[4096,1024]{1,0:T(8,128)}), f32[128,1024]{1,0:T(8,128)}) %reduce-scatter.5.cloned.1.call-update) | async-done | bytes 524304 | tf_op jit(solution)/shard_map/reduce_scatter | solution.py:200
  (260 shorter events, 141.8 us)
Async XLA Ops:
  7.2 63.6 %all-gather.15.cloned.1.call-start = ((), (), s32[]{:S(2)}) async-start(), calls=%async_computation.2 | async-start | bytes 2162688 | tf_op jit(solution)/shard_map/all_gather | solution.py:112
  8.8 120.9 %all-gather.17.cloned.1.call-start = ((), (), s32[]{:S(2)}) async-start(), calls=%async_computation.3 | async-start | bytes 2162688 | tf_op jit(solution)/shard_map/all_gather | solution.py:113
  10.4 178.2 %all-gather.21.cloned.1.call-start = ((), (), s32[]{:S(2)}) async-start(), calls=%async_computation.5 | async-start | bytes 2162688 | tf_op jit(solution)/shard_map/all_gather | solution.py:114
  12.0 206.6 %all-gather.19.cloned.1.call-start = ((), (), s32[]{:S(2)}) async-start(), calls=%async_computation.4 | async-start | bytes 2359296 | tf_op jit(solution)/shard_map/all_gather | solution.py:147
  26.5 171.2 %copy-start.45 = (s32[64]{0:T(128)}, s32[64]{0:T(128)S(1)}, u32[]{:S(2)}) copy-start(s32[64]{0:T(128)S(1)} %iota_add_fusion) | copy-start | bytes 772
  70.8 62.9 %copy-start.2 = (bf16[2,64,1024]{2,1,0:T(8,128)(2,1)S(1)}, bf16[2,64,1024]{2,1,0:T(8,128)(2,1)}, u32[]{:S(2)}) copy-start(bf16[2,64,1024]{2,1,0:T(8,128)(2,1)} %param.17) | copy-start | bytes 786436
  138.8 11.1 copy-start.29
  138.8 11.1 copy-start.31
  139.4 10.5 copy-start.41
  144.1 47.2 %copy-start.26 = (f32[2,64,16]{1,2,0:T(8,128)}, f32[2,64,16]{1,2,0:T(8,128)S(1)}, u32[]{:S(2)}) copy-start(f32[2,64,16]{1,2,0:T(8,128)S(1)} %get-tuple-element.96) | copy-start | bytes 24580
  152.0 41.1 %copy-start.24 = (f32[32,4096]{1,0:T(8,128)S(1)}, f32[32,4096]{1,0:T(8,128)}, u32[]{:S(2)}) copy-start(f32[32,4096]{1,0:T(8,128)} %param.24) | copy-start | bytes 1572868
  152.0 45.9 %copy-start.22 = (bf16[2,64,1024]{2,1,0:T(8,128)(2,1)S(1)}, bf16[2,64,1024]{2,1,0:T(8,128)(2,1)}, u32[]{:S(2)}) copy-start(bf16[2,64,1024]{2,1,0:T(8,128)(2,1)} %get-tuple-element.105) | copy-start | bytes 786436
  153.0 96.3 %all-gather.23.cloned.1.call-start = ((), (), s32[]{:S(2)}) async-start(), calls=%async_computation.6 | async-start | bytes 2359296 | tf_op jit(solution)/shard_map/all_gather | solution.py:148
  191.4 117.3 %all-gather.25.cloned.1.call-start = ((), (), s32[]{:S(2)}) async-start(), calls=%async_computation.7 | async-start | bytes 2162688 | tf_op jit(solution)/shard_map/all_gather | solution.py:115
  193.0 31.8 %copy-start.28 = (f32[2,64,16]{1,2,0:T(8,128)S(1)}, f32[2,64,16]{1,2,0:T(8,128)}, u32[]{:S(2)}) copy-start(f32[2,64,16]{1,2,0:T(8,128)} %copy-done.27) | copy-start | bytes 24580
  193.0 195.4 %all-gather.29.cloned.1.call-start = ((), (), s32[]{:S(2)}) async-start(), calls=%async_computation.9 | async-start | bytes 8650752 | tf_op jit(solution)/shard_map/all_gather | solution.py:117
  193.8 274.2 %all-gather.27.cloned.1.call-start = ((), (), s32[]{:S(2)}) async-start(), calls=%async_computation.8 | async-start | bytes 8650752 | tf_op jit(solution)/shard_map/all_gather | solution.py:116
  195.7 351.3 %all-gather.31.cloned.1.call-start = ((), (), s32[]{:S(2)}) async-start(), calls=%async_computation.10 | async-start | bytes 8650752 | tf_op jit(solution)/shard_map/all_gather | solution.py:118
  197.6 412.1 %all-gather.33.cloned.1.call-start = ((), (), s32[]{:S(2)}) async-start(), calls=%async_computation.11 | async-start | bytes 2359296 | tf_op jit(solution)/shard_map/all_gather | solution.py:247
  198.9 449.9 %all-gather.35.cloned.1.call-start = ((), (), s32[]{:S(2)}) async-start(), calls=%async_computation.12 | async-start | bytes 2359296 | tf_op jit(solution)/shard_map/all_gather | solution.py:248
  258.5 52.8 %copy-start.34 = (f32[1024]{0:T(1024)S(1)}, f32[1024]{0:T(1024)}, u32[]{:S(2)}) copy-start(f32[1024]{0:T(1024)} %param.27) | copy-start | bytes 12292
  259.3 51.6 %copy-start.16 = (bf16[128,1024]{1,0:T(8,128)(2,1)}, bf16[128,1024]{1,0:T(8,128)(2,1)S(1)}, u32[]{:S(2)}) copy-start(bf16[128,1024]{1,0:T(8,128)(2,1)S(1)} %convert_element_type.163) | copy-start | bytes 786436
  312.4 239.9 %copy-start.48 = (f32[128]{0:T(128)}, f32[128]{0:T(128)S(1)}, u32[]{:S(2)}) copy-start(f32[128]{0:T(128)S(1)} %fusion.57) | copy-start | bytes 1540
  553.7 15.8 %slice-start = ((s8[8388608]{0:T(1024)(128)(4,1)}), s8[4194304]{0:T(1024)(128)(4,1)S(1)}, s32[]{:S(2)}) async-start(s8[8388608]{0:T(1024)(128)(4,1)} %bitcast.139), calls=%async_computation.15 | async-start | bytes 8388608
  554.7 14.8 %slice-start.1 = ((s8[8388608]{0:T(1024)(128)(4,1)}), s8[4194304]{0:T(1024)(128)(4,1)S(1)}, s32[]{:S(2)}) async-start(s8[8388608]{0:T(1024)(128)(4,1)} %bitcast.139), calls=%async_computation.16 | async-start | bytes 8388608
  576.1 578.1 %reduce-scatter.3.cloned.1.call-start = ((), (), s32[]{:S(2)}) async-start(), calls=%async_computation.13 | async-start | bytes 51904512 | tf_op jit(solution)/shard_map/reduce_scatter | solution.py:293
  724.8 617.9 %reduce-scatter.5.cloned.1.call-start = ((), (), s32[]{:S(2)}) async-start(), calls=%async_computation.14 | async-start | bytes 17301504 | tf_op jit(solution)/shard_map/reduce_scatter | solution.py:200
  737.3 9.0 copy-start.42
  737.3 9.0 copy-start.43
  737.3 50.4 %copy-start.4 = (bf16[1024,1024]{1,0:T(8,128)(2,1)S(1)}, bf16[1024,1024]{1,0:T(8,128)(2,1)}, u32[]{:S(2)}) copy-start(bf16[1024,1024]{1,0:T(8,128)(2,1)} %all-gather.15.cloned.1.call-done) | copy-start | bytes 6291460
  738.5 49.2 %copy-start.12 = (f32[128,1024]{1,0:T(8,128)S(1)}, f32[128,1024]{1,0:T(8,128)}, u32[]{:S(2)}) copy-start(f32[128,1024]{1,0:T(8,128)} %copy-done.11) | copy-start | bytes 1572868
  746.2 44.3 %copy-start.23 = (bf16[128,1024]{1,0:T(8,128)(2,1)S(1)}, bf16[128,1024]{1,0:T(8,128)(2,1)}, u32[]{:S(2)}) copy-start(bf16[128,1024]{1,0:T(8,128)(2,1)} %convert_element_type.192) | copy-start | bytes 786436
  (42 other events, 197.5 us)
Sparse Core Ops, SparseCore 0:
  11.6 59.1 all-gather.14
  74.3 55.3 all-gather.16
  133.3 55.3 all-gather.20
  190.7 27.9 all-gather.18
  220.7 28.5 all-gather.22
  252.7 55.9 all-gather.24
  312.3 76.1 all-gather.28
  392.0 75.9 all-gather.26
  471.0 75.9 all-gather.30
  548.5 27.6 all-gather.32
  577.8 32.8 all-gather.34
  724.9 429.2 reduce-scatter.2
  1157.0 185.6 reduce-scatter.4
where the time goes:
time: 1360 us; the launch traced here: 1350 us
  waiting for transfers between devices  988 us (73%)
  matrix products  122 us (9%)
  local copies, waits for them, and re-layouts  97.2 us (7%)
  blocking collectives  95.6 us (7%)
  other arithmetic  31.4 us (2%)
  between operations  15.1 us (1%)
    reduce_scatter x1, waiting for transfers between devices, body(): lax.psum_scatter(jnp.concatenate([jnp.concatenate([outer_rows(flat_tokens...  362 us
    reduce_scatter x1, waiting for transfers between devices, body(): lax.psum_scatter(outer_rows(mixed_low, dm_low), ('dp', 'blk'), scatter_di...  184 us
    all_gather x1, waiting for transfers between devices, body(): lax.all_gather(w_gate.astype(jnp.bfloat16), ('dp', 'blk'), axis=0, tiled=...  75.2 us
    all_gather x1, waiting for transfers between devices, body(): lax.all_gather(w_up.astype(jnp.bfloat16), ('dp', 'blk'), axis=0, tiled=True)  73.5 us
    all_gather x1, waiting for transfers between devices, body(): lax.all_gather(w_down.astype(jnp.bfloat16), ('dp', 'blk'), axis=0, tiled=...  71.5 us
    all_gather x1, waiting for transfers between devices, body(): lax.all_gather(w_key.astype(jnp.bfloat16), ('dp', 'blk'), axis=0, tiled=T...  56 us
    all_gather x1, waiting for transfers between devices, body(): lax.all_gather(w_out.astype(jnp.bfloat16), ('dp', 'blk'), axis=0, tiled=T...  49.4 us
    all_gather x1, waiting for transfers between devices, body(): lax.all_gather(w_query.astype(jnp.bfloat16), ('dp', 'blk'), axis=0, tiled...  42.7 us
  transfers between devices with their start and end apart: 13, of which 11 were waited for; matrix products, arithmetic and copies ran while one was open for 12% of the time, Pallas kernels for 0%

commit v1 on v0

v1 whole, which is shorter than its diff:
```python
import math

import jax
import jax.numpy as jnp
from jax import lax
from jax.sharding import Mesh
from jax.sharding import PartitionSpec as P

HEADS = 16
HEAD_DIM = 64
EPS = 1e-06
NEG = -1e30
BF = jnp.bfloat16
F32 = jnp.float32


def dot(a, b):
    return jnp.dot(a, b, preferred_element_type=F32)


def dot_t(a, b):
    return lax.dot_general(a, b, (((1,), (1,)), ((), ())), preferred_element_type=F32)


def tdot(a, b):
    return lax.dot_general(a, b, (((0,), (0,)), ((), ())), preferred_element_type=F32)


def rotate(tensor, cosines, sines):
    half_dim = tensor.shape[-1] // 2
    front = tensor[..., :half_dim]
    behind = tensor[..., half_dim:]
    return jnp.concatenate(
        [front * cosines - behind * sines, behind * cosines + front * sines], axis=-1
    )


def sphere(tensor):
    return tensor * lax.rsqrt(jnp.mean(tensor * tensor, axis=-1, keepdims=True) + EPS)


def head_unit(tensor, gains):
    return gains * tensor * lax.rsqrt(jnp.sum(tensor * tensor, axis=-1, keepdims=True) + EPS)


def residual_step(branch, residual_in, alpha):
    return sphere(residual_in + alpha * (sphere(branch) - residual_in))


def gating(up_proj, gate_proj, scale_up, scale_gate):
    return scale_up * up_proj * jax.nn.silu(scale_gate * gate_proj)


def make_body(sizes):
    ny, nx, nw, nz, nc = sizes
    ndev = ny * nx * nw * nz * nc
    line = ("w", "z")
    nline = nw * nz
    quad = ("x", "z")
    nquad = nx * nz

    def swap(value, axes, count, k):
        return lax.ppermute(value, axes, [(i, i ^ k) for i in range(count)])

    def gather_rel(value, axes, count):
        return [value] + [swap(value, axes, count, k) for k in range(1, count)]

    def exchange_rel(chunks, axes, count):
        return [chunks[0]] + [swap(chunks[k], axes, count, k) for k in range(1, count)]

    def sum_rel(chunks, axes, count):
        got = exchange_rel([c.astype(BF) for c in chunks], axes, count)
        total = chunks[0].astype(F32)
        for piece in got[1:]:
            total = total + piece.astype(F32)
        return total

    def place(pieces, rank):
        stack = jnp.stack(pieces)
        order = rank ^ jnp.arange(len(pieces))
        return jnp.take(stack, order, axis=0)

    def pick(array, rank, count):
        return [lax.dynamic_index_in_dim(array, rank ^ k, 0, False) for k in range(count)]

    def body(
        tokens, doc_ids, w_query, w_key, w_value, w_out, w_up, w_gate, w_down,
        s_qk, alpha_attn, s_up, s_gate, alpha_mlp, cotangent,
    ):
        nseq, seg, dm = tokens.shape
        rows = w_query.shape[0]
        ff = w_up.shape[1]
        ffq = ff // nquad
        ffb = ff // ndev
        hcols = dm // nline
        nheads = HEADS // nline
        score_scale = math.sqrt(HEAD_DIM)
        c_at = lax.axis_index("c")
        line_at = lax.axis_index(line)
        quad_at = lax.axis_index(quad)

        def by_line(w):
            return w.astype(BF).reshape(rows, nline, hcols)

        w_qkv = jnp.stack([by_line(w_query), by_line(w_key), by_line(w_value)], axis=2)
        w_qkv = w_qkv.transpose(1, 0, 2, 3).reshape(nline, rows, 3 * hcols)
        got = place(exchange_rel(pick(w_qkv, line_at, nline), line, nline), line_at)
        full = lax.all_gather(got, ("y", "x", "c"), axis=0)
        full = full.reshape(ny, nx, nc, nw, nz, rows, 3 * hcols).transpose(0, 1, 3, 4, 2, 5, 6)
        full_qkv = full.reshape(dm, 3 * hcols)
        full_out = lax.all_gather(w_out.astype(BF), ("y", "x", "w", "z", "c"), axis=0, tiled=True)

        def by_quad(w):
            w = w.astype(BF).reshape(rows, ny, nx, nw, nz, nc, ffb)
            return w.transpose(2, 4, 0, 1, 3, 5, 6).reshape(nquad, rows, ffq)

        w_ug = jnp.concatenate([by_quad(w_up), by_quad(w_gate)], axis=2)
        got = place(exchange_rel(pick(w_ug, quad_at, nquad), quad, nquad), quad_at)
        full = lax.all_gather(got, ("y", "w", "c"), axis=0)
        full = full.reshape(ny, nw, nc, nx, nz, rows, 2 * ffq).transpose(0, 3, 1, 4, 2, 5, 6)
        full_ug = full.reshape(dm, 2 * ffq)
        full_down = lax.all_gather(w_down.astype(BF), ("y", "w", "c"), axis=0, tiled=True)

        def my_ff(vec):
            v = vec.reshape(ny, nx, nw, nz, nc, ffb).transpose(1, 3, 0, 2, 4, 5)
            return lax.dynamic_index_in_dim(v.reshape(nquad, ffq), quad_at, 0, False)

        my_s_up, my_s_gate = my_ff(s_up), my_ff(s_gate)
        my_gain = lax.dynamic_index_in_dim(s_qk.reshape(nline, hcols), line_at, 0, False)

        def to_row(value):
            keep = lax.dynamic_index_in_dim(value, c_at, 0, False)
            send = lax.dynamic_index_in_dim(value, 1 - c_at, 0, False)
            return jnp.concatenate([keep, lax.ppermute(send, "c", [(0, 1), (1, 0)])], axis=0)

        def from_row(value, send_type):
            keep, send = value[:seg], value[seg:]
            other = lax.ppermute(send.astype(send_type), "c", [(0, 1), (1, 0)])
            pair = jnp.stack([keep, other.astype(value.dtype)])
            return jnp.where(c_at == 0, pair, pair[::-1])

        docs = doc_ids.astype(BF)
        extra = jnp.zeros((nseq, 16, dm), BF).at[:, 0, :seg].set(docs)
        ext = jnp.concatenate([tokens, extra], axis=1)
        mine = to_row(ext).reshape(2, seg + 16, dm)
        everyone = jnp.stack(gather_rel(mine, line, nline))
        row_tokens = everyone[:, :, :seg].reshape(nline * 2 * seg, dm)
        row_docs = everyone[:, :, seg, :seg].reshape(-1).astype(F32)
        peers = line_at ^ jnp.arange(nline)
        seg_at = 2 * peers[:, None] + jnp.stack([c_at, 1 - c_at])[None, :]
        index = (seg_at[:, :, None] * seg + jnp.arange(seg)).reshape(-1)
        start = jnp.sum((row_docs[None, :] < row_docs[:, None]).astype(jnp.int32), axis=1)
        pos = index - start
        allowed = (index[None, :] <= index[:, None]) & (index[None, :] >= start[:, None])
        frequency = 10000.0 ** (-jnp.arange(HEAD_DIM // 2, dtype=F32) / (HEAD_DIM // 2))
        angles = pos.astype(F32)[:, None] * frequency
        cosines, sines = jnp.cos(angles)[:, None, :], jnp.sin(angles)[:, None, :]
        nt = row_tokens.shape[0]
        x_low = mine[:, :seg].reshape(2 * seg, dm)
        x_row = x_low.astype(F32)

        pre = dot(row_tokens, full_qkv)

        def heads(t):
            return t.reshape(nt, nheads, HEAD_DIM)

        def unit_pair(q_pre, k_pre, gains):
            gains = gains.reshape(nheads, HEAD_DIM)
            return (
                head_unit(rotate(heads(q_pre), cosines, sines), gains),
                head_unit(rotate(heads(k_pre), cosines, sines), gains),
            )

        (q_unit, k_unit), unit_pull = jax.vjp(
            unit_pair, pre[:, :hcols], pre[:, hcols : 2 * hcols], my_gain
        )
        q_low, k_low = q_unit.astype(BF), k_unit.astype(BF)
        v_low = heads(pre[:, 2 * hcols :].astype(BF))
        scores = jnp.einsum("qhd,khd->hqk", q_low, k_low, preferred_element_type=F32) * score_scale
        scores = jnp.where(allowed[None], scores, NEG)
        peak = jnp.max(scores, axis=-1, keepdims=True)
        raw = jnp.where(allowed[None], jnp.exp(scores - peak), 0.0)
        probs = raw / jnp.sum(raw, axis=-1, keepdims=True)
        p_low = probs.astype(BF)
        attended = jnp.einsum("hqk,khd->qhd", p_low, v_low, preferred_element_type=F32)
        att_low = attended.astype(BF).reshape(nline, 2 * seg, hcols)
        got = place(exchange_rel([att_low[k] for k in range(nline)], line, nline), line_at)
        att_mine = got.transpose(1, 0, 2).reshape(2 * seg, dm)

        h_attn = dot(att_mine, full_out)
        h_one, attn_pull = jax.vjp(residual_step, h_attn, x_row, alpha_attn)
        h_low = jnp.concatenate(gather_rel(h_one.astype(BF), quad, nquad), axis=0)
        ug = dot(h_low, full_ug)
        mixed, gate_pull = jax.vjp(gating, ug[:, :ffq], ug[:, ffq:], my_s_up, my_s_gate)
        mixed_low = mixed.astype(BF)
        part = dot(mixed_low, full_down).reshape(nquad, 2 * seg, dm)
        h_mlp = sum_rel([part[k] for k in range(nquad)], quad, nquad)
        result, out_pull = jax.vjp(residual_step, h_mlp, h_one, alpha_mlp)
        hidden_out = from_row(result.astype(BF), BF)

        d_result = to_row(cotangent).astype(F32)
        d_hmlp, d_hone, g_alpha_mlp = out_pull(d_result)
        dm_low = jnp.concatenate(gather_rel(d_hmlp.astype(BF), quad, nquad), axis=0)
        d_mixed = dot_t(dm_low, full_down)
        d_up, d_gate, g_s_up, g_s_gate = gate_pull(d_mixed)
        dug_low = jnp.concatenate([d_up.astype(BF), d_gate.astype(BF)], axis=1)
        part = dot_t(dug_low, full_ug).reshape(nquad, 2 * seg, dm)
        d_hone = d_hone + sum_rel([part[k] for k in range(nquad)], quad, nquad)
        g_down = lax.psum_scatter(
            tdot(mixed_low, dm_low).astype(BF), ("y", "w", "c"), scatter_dimension=0, tiled=True
        ).astype(F32)
        g_ug = tdot(h_low, dug_low).astype(BF)
        g_ug = g_ug.reshape(ny, nx, nw, nz, nc, rows, 2 * ffq).transpose(0, 2, 4, 1, 3, 5, 6)
        g_ug = lax.psum_scatter(
            g_ug.reshape(ny * nw * nc, nquad, rows, 2 * ffq),
            ("y", "w", "c"), scatter_dimension=0, tiled=True,
        )[0]
        got = place(exchange_rel(pick(g_ug, quad_at, nquad), quad, nquad), quad_at)
        got = got.reshape(nx, nz, rows, 2, ny, nw, nc, ffb).transpose(3, 2, 4, 0, 5, 1, 6, 7)
        g_up, g_gate = got.reshape(2, rows, ff).astype(F32)

        d_hattn, d_tokens, g_alpha_attn = attn_pull(d_hone)
        dh_low = d_hattn.astype(BF)
        g_out = lax.psum_scatter(
            tdot(att_mine, dh_low).astype(BF), ("y", "x", "w", "z", "c"),
            scatter_dimension=0, tiled=True,
        ).astype(F32)
        d_att = dot_t(dh_low, full_out).astype(BF).reshape(2 * seg, nline, hcols).transpose(1, 0, 2)
        d_att = jnp.concatenate(
            exchange_rel(pick(d_att, line_at, nline), line, nline), axis=0
        ).reshape(nt, nheads, HEAD_DIM)
        delta = jnp.sum(d_att.astype(F32) * attended, axis=-1)
        d_probs = jnp.einsum("qhd,khd->hqk", d_att, v_low, preferred_element_type=F32)
        d_scores = (probs * (d_probs - delta.T[:, :, None])).astype(BF)
        d_q = score_scale * jnp.einsum("hqk,khd->qhd", d_scores, k_low, preferred_element_type=F32)
        d_k = score_scale * jnp.einsum("hqk,qhd->khd", d_scores, q_low, preferred_element_type=F32)
        d_v = jnp.einsum("hqk,qhd->khd", p_low, d_att, preferred_element_type=F32)
        d_qpre, d_kpre, g_sqk = unit_pull((d_q, d_k))
        d_qkv = jnp.concatenate([d_qpre, d_kpre, d_v.reshape(nt, hcols)], axis=1).astype(BF)
        part = dot_t(d_qkv, full_qkv).reshape(nline, 2 * seg, dm)
        tokens_grad = d_tokens + sum_rel([part[k] for k in range(nline)], line, nline)
        tokens_grad = from_row(tokens_grad, BF)
        g_qkv = tdot(row_tokens, d_qkv).astype(BF)
        g_qkv = g_qkv.reshape(ny, nx, nw, nz, nc, rows, 3 * hcols).transpose(0, 1, 4, 2, 3, 5, 6)
        g_qkv = lax.psum_scatter(
            g_qkv.reshape(ny * nx * nc, nline, rows, 3 * hcols),
            ("y", "x", "c"), scatter_dimension=0, tiled=True,
        )[0]
        got = place(exchange_rel(pick(g_qkv, line_at, nline), line, nline), line_at)
        got = got.reshape(nline, rows, 3, hcols).transpose(2, 1, 0, 3).reshape(3, rows, dm)
        g_query, g_key, g_value = got.astype(F32)

        def spread(vec, rank, count):
            return jnp.where(jnp.arange(count)[:, None] == rank, vec[None], 0.0)

        def ff_order(vec):
            v = spread(vec, quad_at, nquad).reshape(nx, nz, ny, nw, nc, ffb)
            return v.transpose(2, 0, 3, 1, 4, 5).reshape(ndev, ffb)

        vecs = jnp.concatenate(
            [
                spread(g_sqk, line_at, nline).reshape(ndev, -1),
                g_alpha_attn.reshape(ndev, -1),
                ff_order(g_s_up),
                ff_order(g_s_gate),
                g_alpha_mlp.reshape(ndev, -1),
            ],
            axis=1,
        )
        vecs = lax.psum_scatter(
            vecs, ("y", "x", "w", "z", "c"), scatter_dimension=0, tiled=True
        )[0]
        cuts = [rows, 2 * rows, 2 * rows + ffb, 2 * rows + 2 * ffb]
        g_sqk, g_alpha_attn, g_s_up, g_s_gate, g_alpha_mlp = jnp.split(vecs, cuts)
        return (
            hidden_out, tokens_grad, g_query, g_key, g_value, g_out, g_up, g_gate, g_down,
            g_sqk, g_alpha_attn, g_s_up, g_s_gate, g_alpha_mlp,
        )

    return body


def solution(mesh):
    ndp, nblk = mesh.shape["dp"], mesh.shape["blk"]
    sizes = (ndp // 2, 2, nblk // 4, 2, 2)
    fine = Mesh(mesh.devices.reshape(sizes), ("y", "x", "w", "z", "c"))
    rows, cols = ("y", "x"), ("w", "z", "c")
    flat = rows + cols
    seq = P(rows, cols, None)
    weight = P(flat, None)
    return jax.shard_map(
        make_body(sizes),
        mesh=fine,
        in_specs=(seq, P(rows, cols)) + (weight,) * 7 + (P(),) * 5 + (seq,),
        out_specs=(seq, seq) + (weight,) * 7 + (P(flat),) * 5,
        check_vma=False,
    )
```

time: 1360 us -> 613 us (0.45)
  waiting for transfers between devices: 988 us -> 380 us
  matrix products: 122 us -> 40.2 us
  starting transfers between devices: 1.06 us -> 56.4 us
  blocking collectives: 95.6 us -> 42.4 us
  local copies, waits for them, and re-layouts: 97.2 us -> 44.5 us
    all_gather x11 -> x4, waiting for transfers between devices: 441 us -> 86.9 us  [the longest x1 48.5 us: body(): full = lax.all_gather(got, ('y', 'w', 'c'), axis=0)]
    reduce_scatter x2 -> x4, waiting for transfers between devices: 547 us -> 212 us  [the longest x1 137 us: body(): lax.psum_scatter(tdot(att_mine, dh_low).astype(BF), ('y', 'x', 'w', 'z',...]
    dot_general x27 -> x17, matrix products: 122 us -> 36.3 us  [the longest x4 10.7 us: dot(): return jnp.dot(a, b, preferred_element_type=F32)]
    ppermute x0 -> x40, waiting for transfers between devices: none -> 80.8 us  [the longest x36 79.5 us: swap(): return lax.ppermute(value, axes, [(i, i ^ k) for i in range(count)])]
    all_gather x4 -> x0, blocking collectives: 57 us -> none  [the longest x1 17.1 us: body(): lax.all_gather(log_total, 'blk', axis=2, tiled=True)]
    ppermute x0 -> x40, starting transfers between devices: none -> 55.5 us  [the longest x36 55.2 us: swap(): return lax.ppermute(value, axes, [(i, i ^ k) for i in range(count)])]
    dot_general x5 -> x0, local copies, waits for them, and re-layouts: 23.2 us -> none  [the longest x3 16.3 us: outer_rows(): jnp.einsum('tr,tc->rc', left, right, preferred_element_type=jnp.float32)]
    all_gather x6 -> x0, local copies, waits for them, and re-layouts: 22.3 us -> none  [the longest x1 6.15 us: body(): query_rows = lax.all_gather(q_low, 'blk', axis=1, tiled=True)]
  transfers between devices with their start and end apart: 13 -> 48, of which waited for: 11 -> 23; matrix products, arithmetic and copies ran while one was open for 12% -> 11% of each run, Pallas kernels for 0% -> 0%
where the time goes in v1:
time: 613 us; the launch traced here: 609 us
  waiting for transfers between devices  380 us (62%)
  starting transfers between devices  56.4 us (9%)
  local copies, waits for them, and re-layouts  44.5 us (7%)
  blocking collectives  42.4 us (7%)
  matrix products  40.2 us (7%)
  other arithmetic  29.1 us (5%)
  between operations  16.3 us (3%)
    reduce_scatter x1, waiting for transfers between devices, body(): lax.psum_scatter(tdot(att_mine, dh_low).astype(BF), ('y', 'x', 'w', 'z',...  137 us
    ppermute x36, waiting for transfers between devices, swap(): return lax.ppermute(value, axes, [(i, i ^ k) for i in range(count)])  79.5 us
    ppermute x36, starting transfers between devices, swap(): return lax.ppermute(value, axes, [(i, i ^ k) for i in range(count)])  55.2 us
    all_gather x1, waiting for transfers between devices, body(): full = lax.all_gather(got, ('y', 'w', 'c'), axis=0)  48.5 us
    reduce_scatter x1, waiting for transfers between devices, body(): lax.psum_scatter(tdot(mixed_low, dm_low).astype(BF), ('y', 'w', 'c'), sca...  45.8 us
    unnamed x1, blocking collectives  42.4 us
    reduce_scatter x1, waiting for transfers between devices, body(): lax.psum_scatter(g_ug.reshape(ny * nw * nc, nquad, rows, 2 * ffq), ('y',...  29.5 us
    all_gather x1, waiting for transfers between devices, body(): lax.all_gather(w_down.astype(BF), ('y', 'w', 'c'), axis=0, tiled=True)  28 us
  transfers between devices with their start and end apart: 48, of which 23 were waited for; matrix products, arithmetic and copies ran while one was open for 11% of the time, Pallas kernels for 0%

profile of v1, /device:TPU:0, one launch (start us, length us, event | category | flops | bytes accessed | tf_op | source)
XLA Modules:
  0.0 608.6 jit_solution(3294106817460965763)
XLA Ops:
  11.3 3.1 collective-permute-start.4
  14.4 2.6 collective-permute-start.5
  17.0 3.3 collective-permute-done.5
  20.3 2.6 collective-permute-done.6
  42.7 10.2 %collective-permute-done.1 = bf16[2,80,1024]{2,1,0:T(8,128)(2,1)S(1)} collective-permute-done((bf16[2,80,1024]{2,1,0:T(8,128)(2,1)S(1)}, bf16[2,80,1024]{2,1,0:T(8,128)(2,1)S(1)}, u32[]{:S(2)}, u32[]{:S(2)}) %collective-permute-start.1) | collective-permute-done | bytes 327712 | tf_op jit(solution)/shard_map/ppermute | solution.py:63
  52.9 12.2 %collective-permute-done.2 = bf16[2,80,1024]{2,1,0:T(8,128)(2,1)S(1)} collective-permute-done((bf16[2,80,1024]{2,1,0:T(8,128)(2,1)S(1)}, bf16[2,80,1024]{2,1,0:T(8,128)(2,1)S(1)}, u32[]{:S(2)}, u32[]{:S(2)}) %collective-permute-start.2) | collective-permute-done | bytes 327712 | tf_op jit(solution)/shard_map/ppermute | solution.py:63
  72.8 4.0 fusion.55
  76.8 2.8 fusion.8
  82.2 8.1 %collective-permute-start.7 = (bf16[128,256]{0,1:T(8,128)(2,1)S(1)}, bf16[128,256]{0,1:T(8,128)(2,1)S(1)}, u32[]{:S(2)}, u32[]{:S(2)}) collective-permute-start(bf16[128,256]{0,1:T(8,128)(2,1)S(1)} %bitcast.255), channel_id=1, source_target_pairs={{0,2},{2,0},{4,6},{6,4},{1,3},{3,1},{5,7},{7,5},{8,10},{10,8},{12,... | collective-permute-start | bytes 196616 | tf_op jit(solution)/shard_map/ppermute | solution.py:63
  93.5 4.4 collective-permute-done.8
  98.7 10.4 %all-gather.7.cloned.1.call-done = bf16[1024,1024]{1,0:T(8,128)(2,1)} async-done(((bf16[32,1024]{1,0:T(8,128)(2,1)}), bf16[1024,1024]{1,0:T(8,128)(2,1)}) %all-gather.7.cloned.1.call-update) | async-done | bytes 2097168 | tf_op jit(solution)/shard_map/all_gather | solution.py:111
  117.0 48.5 %all-gather.13.cloned.1.call-done = bf16[32,32,2048]{2,1,0:T(8,128)(2,1)} async-done(((bf16[4,32,2048]{2,1,0:T(8,128)(2,1)}), bf16[32,32,2048]{2,1,0:T(8,128)(2,1)}) %all-gather.13.cloned.1.call-update) | async-done | bytes 4194320 | tf_op jit(solution)/shard_map/all_gather | solution.py:119
  168.0 4.4 fusion.27
  176.1 28.0 %all-gather.9.cloned.1.call-done = bf16[1024,1024]{1,0:T(8,128)(2,1)} async-done(((bf16[128,1024]{1,0:T(8,128)(2,1)}), bf16[1024,1024]{1,0:T(8,128)(2,1)}) %all-gather.9.cloned.1.call-update) | async-done | bytes 2097168 | tf_op jit(solution)/shard_map/all_gather | solution.py:122
  204.0 3.2 fusion.57
  211.0 5.5 collective-permute-done.16
  216.5 5.9 collective-permute-done.18
  228.9 5.8 collective-permute-done.21
  234.7 4.4 collective-permute-done.22
  239.1 3.0 multiply_reduce_fusion
  248.5 5.7 collective-permute-done.24
  254.2 4.0 collective-permute-done.25
  274.0 2.9 collective-permute-done.29
  279.7 3.1 multiply_convert_fusion
  289.7 3.6 convolution_convert_fusion
  297.2 2.6 convolution_convert_fusion.1
  306.1 3.0 collective-permute-start.31
  310.7 42.4 %all-reduce.5 = f32[32,352]{1,0:T(8,128)S(1)} all-reduce(f32[32,352]{1,0:T(8,128)S(1)} %concatenate.63), channel_id=8, replica_groups=mesh['y'=2,'x'=2,'w'=2,'z'=2,'c'=2] {'y','x','w','z','c'}, use_global_device_ids=true, to_apply=%region_26.29.clone | all-reduce | flops 11264 | bytes 90112
  364.1 8.7 %collective-permute-done.35 = bf16[32,768]{1,0:T(8,128)(2,1)S(1)} collective-permute-done((bf16[32,768]{1,0:T(8,128)(2,1)S(1)}, bf16[32,768]{1,0:T(8,128)(2,1)S(1)}, u32[]{:S(2)}, u32[]{:S(2)}) %collective-permute-start.35) | collective-permute-done | bytes 49184 | tf_op jit(solution)/shard_map/ppermute | solution.py:63
  373.9 29.5 %reduce-scatter.9.cloned.1.call-done = bf16[1,4,32,2048]{3,2,1,0:T(8,128)(2,1)} async-done(((bf16[8,4,32,2048]{3,2,1,0:T(8,128)(2,1)}), bf16[1,4,32,2048]{3,2,1,0:T(8,128)(2,1)}) %reduce-scatter.9.cloned.1.call-update) | async-done | bytes 524304 | tf_op jit(solution)/shard_map/reduce_scatter | solution.py:214
  410.7 45.8 %reduce-scatter.11.cloned.1.call-done = bf16[128,1024]{1,0:T(8,128)(2,1)} async-done(((bf16[1024,1024]{1,0:T(8,128)(2,1)}), bf16[128,1024]{1,0:T(8,128)(2,1)}) %reduce-scatter.11.cloned.1.call-update) | async-done | bytes 262160 | tf_op jit(solution)/shard_map/reduce_scatter | solution.py:209
  458.3 136.5 %reduce-scatter.7.cloned.1.call-done = bf16[32,1024]{1,0:T(8,128)(2,1)} async-done(((bf16[1024,1024]{1,0:T(8,128)(2,1)}), bf16[32,1024]{1,0:T(8,128)(2,1)}) %reduce-scatter.7.cloned.1.call-update) | async-done | bytes 65552 | tf_op jit(solution)/shard_map/reduce_scatter | solution.py:224
  (438 shorter events, 132.4 us)
Async XLA Ops:
  7.2 60.2 %all-gather.11.cloned.1.call-start = ((), (), s32[]{:S(2)}) async-start(), calls=%async_computation.10 | async-start | bytes 1769472 | tf_op jit(solution)/shard_map/all_gather | solution.py:108
  24.2 84.8 %all-gather.7.cloned.1.call-start = ((), (), s32[]{:S(2)}) async-start(), calls=%async_computation.4 | async-start | bytes 2162688 | tf_op jit(solution)/shard_map/all_gather | solution.py:111
  25.0 140.5 %all-gather.13.cloned.1.call-start = ((), (), s32[]{:S(2)}) async-start(), calls=%async_computation.11 | async-start | bytes 4718592 | tf_op jit(solution)/shard_map/all_gather | solution.py:119
  35.6 168.4 %all-gather.9.cloned.1.call-start = ((), (), s32[]{:S(2)}) async-start(), calls=%async_computation.5 | async-start | bytes 2359296 | tf_op jit(solution)/shard_map/all_gather | solution.py:122
  36.7 321.2 %reduce-scatter.5.cloned.1.call-start = ((), (), s32[]{:S(2)}) async-start(), calls=%async_computation.6 | async-start | bytes 1769472 | tf_op jit(solution)/shard_map/reduce_scatter | solution.py:245
  37.4 15.4 %collective-permute-start.1 = (bf16[2,80,1024]{2,1,0:T(8,128)(2,1)S(1)}, bf16[2,80,1024]{2,1,0:T(8,128)(2,1)S(1)}, u32[]{:S(2)}, u32[]{:S(2)}) collective-permute-start(bf16[2,80,1024]{2,1,0:T(8,128)(2,1)S(1)} %bitcast.194), channel_id=1, source_target_pairs={{0,2},{2,0},{4,6},{6,4},{1,3},{3,1},{5,7},{7,5},{8,10},{10,8},{12,... | collective-permute-start | bytes 983048 | tf_op jit(solution)/shard_map/ppermute | solution.py:63
  39.4 25.6 %collective-permute-start.2 = (bf16[2,80,1024]{2,1,0:T(8,128)(2,1)S(1)}, bf16[2,80,1024]{2,1,0:T(8,128)(2,1)S(1)}, u32[]{:S(2)}, u32[]{:S(2)}) collective-permute-start(bf16[2,80,1024]{2,1,0:T(8,128)(2,1)S(1)} %bitcast.195), channel_id=1, source_target_pairs={{0,4},{2,6},{4,0},{6,2},{1,5},{3,7},{5,1},{7,3},{8,12},{10,14},{12... | collective-permute-start | bytes 983048 | tf_op jit(solution)/shard_map/ppermute | solution.py:63
  39.7 25.4 %collective-permute-start.3 = (bf16[2,80,1024]{2,1,0:T(8,128)(2,1)S(1)}, bf16[2,80,1024]{2,1,0:T(8,128)(2,1)S(1)}, u32[]{:S(2)}, u32[]{:S(2)}) collective-permute-start(bf16[2,80,1024]{2,1,0:T(8,128)(2,1)S(1)} %bitcast.196), channel_id=1, source_target_pairs={{0,6},{2,4},{4,2},{6,0},{1,7},{3,5},{5,3},{7,1},{8,14},{10,12},{12... | collective-permute-start | bytes 983048 | tf_op jit(solution)/shard_map/ppermute | solution.py:63
  82.2 11.3 %collective-permute-start.7 = (bf16[128,256]{0,1:T(8,128)(2,1)S(1)}, bf16[128,256]{0,1:T(8,128)(2,1)S(1)}, u32[]{:S(2)}, u32[]{:S(2)}) collective-permute-start(bf16[128,256]{0,1:T(8,128)(2,1)S(1)} %bitcast.255), channel_id=1, source_target_pairs={{0,2},{2,0},{4,6},{6,4},{1,3},{3,1},{5,7},{7,5},{8,10},{10,8},{12,... | collective-permute-start | bytes 196616 | tf_op jit(solution)/shard_map/ppermute | solution.py:63
  113.3 54.7 %collective-permute-start.10 = (bf16[128,1024]{1,0:T(8,128)(2,1)}, bf16[128,1024]{1,0:T(8,128)(2,1)}, u32[]{:S(2)}, u32[]{:S(2)}) collective-permute-start(bf16[128,1024]{1,0:T(8,128)(2,1)} %multiply_convert_fusion.7), channel_id=1, source_target_pairs={{0,2},{2,0},{8,10},{10,8},{1,3},{3,1},{9,11},{11,9},{4,6},{6,4},{1... | collective-permute-start | bytes 786440 | tf_op jit(solution)/shard_map/ppermute | solution.py:63
  114.0 54.0 %collective-permute-start.11 = (bf16[128,1024]{1,0:T(8,128)(2,1)}, bf16[128,1024]{1,0:T(8,128)(2,1)}, u32[]{:S(2)}, u32[]{:S(2)}) collective-permute-start(bf16[128,1024]{1,0:T(8,128)(2,1)} %multiply_convert_fusion.7), channel_id=1, source_target_pairs={{0,8},{2,10},{8,0},{10,2},{1,9},{3,11},{9,1},{11,3},{4,12},{6,14},... | collective-permute-start | bytes 786440 | tf_op jit(solution)/shard_map/ppermute | solution.py:63
  115.3 52.8 %collective-permute-start.12 = (bf16[128,1024]{1,0:T(8,128)(2,1)}, bf16[128,1024]{1,0:T(8,128)(2,1)}, u32[]{:S(2)}, u32[]{:S(2)}) collective-permute-start(bf16[128,1024]{1,0:T(8,128)(2,1)} %multiply_convert_fusion.7), channel_id=1, source_target_pairs={{0,10},{2,8},{8,2},{10,0},{1,11},{3,9},{9,3},{11,1},{4,14},{6,12},... | collective-permute-start | bytes 786440 | tf_op jit(solution)/shard_map/ppermute | solution.py:63
  208.9 13.4 %collective-permute-start.18 = (bf16[128,1024]{1,0:T(8,128)(2,1)S(1)}, bf16[128,1024]{1,0:T(8,128)(2,1)S(1)}, u32[]{:S(2)}, u32[]{:S(2)}) collective-permute-start(bf16[128,1024]{1,0:T(8,128)(2,1)S(1)} %get-tuple-element.61), channel_id=1, source_target_pairs={{0,10},{2,8},{8,2},{10,0},{1,11},{3,9},{9,3},{11,1},{4,14},{6,12},... | collective-permute-start | bytes 786440 | tf_op jit(solution)/shard_map/ppermute | solution.py:63
  210.9 11.7 %collective-permute-start.20 = (bf16[64,1024]{1,0:T(8,128)(2,1)S(1)}, bf16[64,1024]{1,0:T(8,128)(2,1)S(1)}, u32[]{:S(2)}, u32[]{:S(2)}) collective-permute-start(bf16[64,1024]{1,0:T(8,128)(2,1)S(1)} %get-tuple-element.96), channel_id=1, source_target_pairs={{0,1},{1,0},{2,3},{3,2},{4,5},{5,4},{6,7},{7,6},{8,9},{9,8},{10,11... | collective-permute-start | bytes 393224 | tf_op jit(solution)/shard_map/ppermute | solution.py:134
  225.4 9.3 %collective-permute-start.21 = (bf16[128,1024]{1,0:T(8,128)(2,1)S(1)}, bf16[128,1024]{1,0:T(8,128)(2,1)S(1)}, u32[]{:S(2)}, u32[]{:S(2)}) collective-permute-start(bf16[128,1024]{1,0:T(8,128)(2,1)S(1)} %fusion.12), channel_id=1, source_target_pairs={{0,2},{2,0},{8,10},{10,8},{1,3},{3,1},{9,11},{11,9},{4,6},{6,4},{1... | collective-permute-start | bytes 786440 | tf_op jit(solution)/shard_map/ppermute | solution.py:63
  226.3 12.8 %collective-permute-start.22 = (bf16[128,1024]{1,0:T(8,128)(2,1)S(1)}, bf16[128,1024]{1,0:T(8,128)(2,1)S(1)}, u32[]{:S(2)}, u32[]{:S(2)}) collective-permute-start(bf16[128,1024]{1,0:T(8,128)(2,1)S(1)} %fusion.12), channel_id=1, source_target_pairs={{0,8},{2,10},{8,0},{10,2},{1,9},{3,11},{9,1},{11,3},{4,12},{6,14},... | collective-permute-start | bytes 786440 | tf_op jit(solution)/shard_map/ppermute | solution.py:63
  227.7 11.3 %collective-permute-start.23 = (bf16[128,1024]{1,0:T(8,128)(2,1)S(1)}, bf16[128,1024]{1,0:T(8,128)(2,1)S(1)}, u32[]{:S(2)}, u32[]{:S(2)}) collective-permute-start(bf16[128,1024]{1,0:T(8,128)(2,1)S(1)} %fusion.12), channel_id=1, source_target_pairs={{0,10},{2,8},{8,2},{10,0},{1,11},{3,9},{9,3},{11,1},{4,14},{6,12},... | collective-permute-start | bytes 786440 | tf_op jit(solution)/shard_map/ppermute | solution.py:63
  244.9 9.2 %collective-permute-start.24 = (bf16[128,1024]{1,0:T(8,128)(2,1)S(1)}, bf16[128,1024]{1,0:T(8,128)(2,1)S(1)}, u32[]{:S(2)}, u32[]{:S(2)}) collective-permute-start(bf16[128,1024]{1,0:T(8,128)(2,1)S(1)} %get-tuple-element.57), channel_id=1, source_target_pairs={{0,2},{2,0},{8,10},{10,8},{1,3},{3,1},{9,11},{11,9},{4,6},{6,4},{1... | collective-permute-start | bytes 786440 | tf_op jit(solution)/shard_map/ppermute | solution.py:63
  246.4 11.8 %collective-permute-start.25 = (bf16[128,1024]{1,0:T(8,128)(2,1)S(1)}, bf16[128,1024]{1,0:T(8,128)(2,1)S(1)}, u32[]{:S(2)}, u32[]{:S(2)}) collective-permute-start(bf16[128,1024]{1,0:T(8,128)(2,1)S(1)} %get-tuple-element.59), channel_id=1, source_target_pairs={{0,8},{2,10},{8,0},{10,2},{1,9},{3,11},{9,1},{11,3},{4,12},{6,14},... | collective-permute-start | bytes 786440 | tf_op jit(solution)/shard_map/ppermute | solution.py:63
  247.0 11.2 %collective-permute-start.26 = (bf16[128,1024]{1,0:T(8,128)(2,1)S(1)}, bf16[128,1024]{1,0:T(8,128)(2,1)S(1)}, u32[]{:S(2)}, u32[]{:S(2)}) collective-permute-start(bf16[128,1024]{1,0:T(8,128)(2,1)S(1)} %get-tuple-element.58), channel_id=1, source_target_pairs={{0,10},{2,8},{8,2},{10,0},{1,11},{3,9},{9,3},{11,1},{4,14},{6,12},... | collective-permute-start | bytes 786440 | tf_op jit(solution)/shard_map/ppermute | solution.py:63
  289.0 114.4 %reduce-scatter.9.cloned.1.call-start = ((), (), s32[]{:S(2)}) async-start(), calls=%async_computation.8 | async-start | bytes 4718592 | tf_op jit(solution)/shard_map/reduce_scatter | solution.py:214
  295.6 160.8 %reduce-scatter.11.cloned.1.call-start = ((), (), s32[]{:S(2)}) async-start(), calls=%async_computation.9 | async-start | bytes 2359296 | tf_op jit(solution)/shard_map/reduce_scatter | solution.py:209
  299.9 294.9 %reduce-scatter.7.cloned.1.call-start = ((), (), s32[]{:S(2)}) async-start(), calls=%async_computation.7 | async-start | bytes 2162688 | tf_op jit(solution)/shard_map/reduce_scatter | solution.py:224
  303.5 50.8 %collective-permute-start.19 = (bf16[64,1024]{1,0:T(8,128)(2,1)S(1)}, bf16[64,1024]{1,0:T(8,128)(2,1)S(1)}, u32[]{:S(2)}, u32[]{:S(2)}) collective-permute-start(bf16[64,1024]{1,0:T(8,128)(2,1)S(1)} %get-tuple-element.90), channel_id=1, source_target_pairs={{0,1},{1,0},{2,3},{3,2},{4,5},{5,4},{6,7},{7,6},{8,9},{9,8},{10,11... | collective-permute-start | bytes 393224 | tf_op jit(solution)/shard_map/ppermute | solution.py:138
  306.1 49.0 %collective-permute-start.30 = (bf16[128,1024]{1,0:T(8,128)(2,1)S(1)}, bf16[128,1024]{1,0:T(8,128)(2,1)S(1)}, u32[]{:S(2)}, u32[]{:S(2)}) collective-permute-start(bf16[128,1024]{1,0:T(8,128)(2,1)S(1)} %get-tuple-element.54), channel_id=1, source_target_pairs={{0,2},{2,0},{4,6},{6,4},{1,3},{3,1},{5,7},{7,5},{8,10},{10,8},{12,... | collective-permute-start | bytes 786440 | tf_op jit(solution)/shard_map/ppermute | solution.py:63
  306.1 49.0 %collective-permute-start.31 = (bf16[128,1024]{1,0:T(8,128)(2,1)S(1)}, bf16[128,1024]{1,0:T(8,128)(2,1)S(1)}, u32[]{:S(2)}, u32[]{:S(2)}) collective-permute-start(bf16[128,1024]{1,0:T(8,128)(2,1)S(1)} %get-tuple-element.56), channel_id=1, source_target_pairs={{0,4},{2,6},{4,0},{6,2},{1,5},{3,7},{5,1},{7,3},{8,12},{10,14},{12... | collective-permute-start | bytes 786440 | tf_op jit(solution)/shard_map/ppermute | solution.py:63
  309.1 46.0 %collective-permute-start.32 = (bf16[128,1024]{1,0:T(8,128)(2,1)S(1)}, bf16[128,1024]{1,0:T(8,128)(2,1)S(1)}, u32[]{:S(2)}, u32[]{:S(2)}) collective-permute-start(bf16[128,1024]{1,0:T(8,128)(2,1)S(1)} %get-tuple-element.55), channel_id=1, source_target_pairs={{0,6},{2,4},{4,2},{6,0},{1,7},{3,5},{5,3},{7,1},{8,14},{10,12},{12... | collective-permute-start | bytes 786440 | tf_op jit(solution)/shard_map/ppermute | solution.py:63
  358.9 13.9 %collective-permute-start.35 = (bf16[32,768]{1,0:T(8,128)(2,1)S(1)}, bf16[32,768]{1,0:T(8,128)(2,1)S(1)}, u32[]{:S(2)}, u32[]{:S(2)}) collective-permute-start(bf16[32,768]{1,0:T(8,128)(2,1)S(1)} %get-tuple-element.99), channel_id=1, source_target_pairs={{0,4},{2,6},{4,0},{6,2},{1,5},{3,7},{5,1},{7,3},{8,12},{10,14},{12... | collective-permute-start | bytes 147464 | tf_op jit(solution)/shard_map/ppermute | solution.py:63
  361.0 11.9 %collective-permute-start.36 = (bf16[32,768]{1,0:T(8,128)(2,1)S(1)}, bf16[32,768]{1,0:T(8,128)(2,1)S(1)}, u32[]{:S(2)}, u32[]{:S(2)}) collective-permute-start(bf16[32,768]{1,0:T(8,128)(2,1)S(1)} %get-tuple-element.98), channel_id=1, source_target_pairs={{0,6},{2,4},{4,2},{6,0},{1,7},{3,5},{5,3},{7,1},{8,14},{10,12},{12... | collective-permute-start | bytes 147464 | tf_op jit(solution)/shard_map/ppermute | solution.py:63
  404.5 191.8 %collective-permute-start.37 = (bf16[32,2048]{1,0:T(8,128)(2,1)S(1)}, bf16[32,2048]{1,0:T(8,128)(2,1)S(1)}, u32[]{:S(2)}, u32[]{:S(2)}) collective-permute-start(bf16[32,2048]{1,0:T(8,128)(2,1)S(1)} %get-tuple-element.75), channel_id=1, source_target_pairs={{0,2},{2,0},{8,10},{10,8},{1,3},{3,1},{9,11},{11,9},{4,6},{6,4},{1... | collective-permute-start | bytes 393224 | tf_op jit(solution)/shard_map/ppermute | solution.py:63
  404.6 191.7 %collective-permute-start.38 = (bf16[32,2048]{1,0:T(8,128)(2,1)S(1)}, bf16[32,2048]{1,0:T(8,128)(2,1)S(1)}, u32[]{:S(2)}, u32[]{:S(2)}) collective-permute-start(bf16[32,2048]{1,0:T(8,128)(2,1)S(1)} %get-tuple-element.74), channel_id=1, source_target_pairs={{0,8},{2,10},{8,0},{10,2},{1,9},{3,11},{9,1},{11,3},{4,12},{6,14},... | collective-permute-start | bytes 393224 | tf_op jit(solution)/shard_map/ppermute | solution.py:63
  406.1 190.2 %collective-permute-start.39 = (bf16[32,2048]{1,0:T(8,128)(2,1)S(1)}, bf16[32,2048]{1,0:T(8,128)(2,1)S(1)}, u32[]{:S(2)}, u32[]{:S(2)}) collective-permute-start(bf16[32,2048]{1,0:T(8,128)(2,1)S(1)} %get-tuple-element.73), channel_id=1, source_target_pairs={{0,10},{2,8},{8,2},{10,0},{1,11},{3,9},{9,3},{11,1},{4,14},{6,12},... | collective-permute-start | bytes 393224 | tf_op jit(solution)/shard_map/ppermute | solution.py:63
  (104 other events, 1081.7 us)
Sparse Core Ops, SparseCore 0:
  24.3 24.1 all-gather.10
  52.1 56.8 all-gather.6
  111.5 53.9 all-gather.12
  167.8 36.1 all-gather.8
  289.1 37.9 reduce-scatter.4
  330.3 73.0 reduce-scatter.8
  407.0 49.4 reduce-scatter.10
  458.7 135.9 reduce-scatter.6
